TPU v7x, 256 devices: a whole 4x4x8 slice. The times are simulated.
256 devices in a mesh: fsdp: 4 (over x), expert: 8 (over z), tensor: 8 (over y, core).
Axes of the slice: x: 4, y: 4, z: 8, core: 2. Of those that a mesh axis runs over, the one named last changes fastest.
Arguments:
- tokens: bfloat16 [2, 512, 4096], P(None, 'expert'), may hold values from -6 to 6
- route: int32 [2, 512, 2], P(None, 'expert'), may hold values from 0 to 7, all different within a row; in each aligned block of 64 rows (0 to 63, 64 to 127, ..., all dimensions but the last counted through in order) at most 32 rows name the same one
- route_weight: float32 [2, 512, 2], P(None, 'expert'), may hold values from 0.1 to 1
- gate_up: bfloat16 [8, 2, 4096, 8192], P('expert', None, None, ('fsdp', 'tensor')), may hold values from -0.09375 to 0.09375
- down_weight: bfloat16 [8, 8192, 4096], P('expert', ('fsdp', 'tensor')), may hold values from -0.125 to 0.125
- adam_first: float32 [8, 2048, 4096], P(None, ('fsdp', 'tensor'), 'expert'), may hold values from -2.5 to 2.5
- adam_second: float32 [8, 2048, 4096], P(None, ('fsdp', 'tensor'), 'expert'), may hold values from 0.05 to 1
- gradient: bfloat16 [8, 2048, 4096], P(None, ('fsdp', 'tensor'), 'expert'), may hold values from -6 to 6
- block_list: int32 [8, 32, 4], P(None, ('fsdp', 'tensor')), may hold values from 0 to 7, as said below
- block_count: int32 [8, 32], P(None, ('fsdp', 'tensor')), may hold values from 1 to 4, as said below
Outputs:
- mixed: bfloat16 [2, 512, 4096], P(None, 'expert', ('fsdp', 'tensor'))
- first_new: float32 [8, 2048, 4096], P(None, ('fsdp', 'tensor'), 'expert')
- second_new: float32 [8, 2048, 4096], P(None, ('fsdp', 'tensor'), 'expert')
Inputs may be any that keep to these rules, and one draw needn't show every extreme that they name: `route`: the two experts of a token differ; in each aligned block of 64 tokens of one step no expert is named more than 32 times. `block_list`: the 4 entries of one list are distinct block numbers; only the first block_count entries are applied. `block_count`: 4 is reached in every draw.
All inputs are finite; a program needn't handle non-finite values.
Results may differ from a plain program's by a relative error of at most 0.023.
Values may be sent and summed in bfloat16 or wider, within the bound.
A program may use at most 64 MiB of HBM per device.

v0:
```python
import jax
import jax.numpy as jnp
from jax import lax
from jax.sharding import PartitionSpec as P

E = 8
STRIDE = 4
BLOCK_ROWS = 8
MAXCH = 4
S = 2
CAP = 32


BETA_ONE = 0.9
BETA_TWO = 0.95
LEARN_RATE = 0.03
ADAM_EPS = 1e-08
FIRST_FIX = 1.0 - 0.9**10
SECOND_FIX = 1.0 - 0.95**10


def adam_moments(adam_first, adam_second, gradient):
    grad_wide = gradient.astype(jnp.float32)
    first_new = BETA_ONE * adam_first + (1.0 - BETA_ONE) * grad_wide
    second_new = BETA_TWO * adam_second + (1.0 - BETA_TWO) * grad_wide * grad_wide
    step_size = (
        LEARN_RATE * (first_new / FIRST_FIX) / (jnp.sqrt(second_new / SECOND_FIX) + ADAM_EPS)
    )
    return (first_new, second_new, (-step_size).astype(jnp.bfloat16))


def on_device(
    tokens,
    route,
    route_weight,
    gate_up,
    down_weight,
    adam_first,
    adam_second,
    gradient,
    block_list,
    block_count,
):
    first_new, second_new, delta = adam_moments(adam_first, adam_second, gradient)
    groups = lax.axis_size("expert")
    owned_experts = gate_up.shape[0]
    shard_rows = delta.shape[1]
    block_total = shard_rows // BLOCK_ROWS
    width = down_weight.shape[2]
    expert_start = lax.axis_index("expert") * owned_experts
    own_list = lax.dynamic_slice_in_dim(block_list[:, 0, :], expert_start, owned_experts, 0)
    own_count = lax.dynamic_slice_in_dim(block_count[:, 0], expert_start, owned_experts, 0)
    listed = jnp.arange(MAXCH)[None, :] < own_count[:, None]
    picked = (own_list[:, :, None] == jnp.arange(block_total)[None, None, :]) & listed[:, :, None]
    row_mask = jnp.repeat(jnp.any(picked, axis=1), BLOCK_ROWS, axis=1)
    incoming = lax.all_to_all(delta, "expert", split_axis=0, concat_axis=2, tiled=True)
    strided = down_weight.reshape(owned_experts, shard_rows, STRIDE, width)
    fresh_rows = (
        strided[:, :, 0, :].astype(jnp.float32)
        + jnp.where(row_mask[:, :, None], incoming.astype(jnp.float32), 0.0)
    ).astype(jnp.bfloat16)
    down_new = jnp.concatenate([fresh_rows[:, :, None, :], strided[:, :, 1:, :]], axis=2).reshape(
        owned_experts, shard_rows * STRIDE, width
    )
    slots_all = CAP * E
    shards = lax.axis_size(("fsdp", "tensor"))
    group_index = lax.axis_index(("fsdp", "tensor"))
    my_rows = slots_all // shards
    token_count = tokens.shape[1]
    outputs = []
    for decode_step in range(S):
        token_rows = tokens[decode_step]
        pair_expert = route[decode_step].reshape(-1)
        onehot = (pair_expert[:, None] == jnp.arange(E)[None, :]).astype(jnp.int32)
        position = jnp.sum((jnp.cumsum(onehot, axis=0) - onehot) * onehot, axis=1)
        slot_index = position * E + pair_expert
        placed = (slot_index[:, None] == jnp.arange(slots_all)[None, :]).reshape(
            token_count, 2, slots_all
        )
        selector = jnp.sum(placed.astype(jnp.int32), axis=1).astype(jnp.bfloat16)
        gathered = lax.dot_general(
            selector, token_rows, (((0,), (0,)), ((), ())), preferred_element_type=jnp.float32
        )
        outgoing = gathered.astype(jnp.bfloat16).reshape(CAP, E, 1, width)
        received = lax.all_to_all(outgoing, "expert", split_axis=1, concat_axis=2, tiled=True)
        flat_rows = received.reshape(slots_all, width)
        weights = route_weight[decode_step].reshape(-1)
        slot_block = flat_rows.reshape(slots_all // E, owned_experts, groups, width)
        projected = jnp.einsum(
            "cxed,xgdh->cxegh", slot_block, gate_up, preferred_element_type=jnp.float32
        )
        hidden = (jax.nn.silu(projected[:, :, :, 0, :]) * projected[:, :, :, 1, :]).astype(
            jnp.bfloat16
        )
        down_term = jnp.einsum(
            "cxeh,xhd->cxed", hidden, down_new, preferred_element_type=jnp.float32
        )
        rounded = lax.optimization_barrier(down_term.astype(jnp.bfloat16))
        summed_all = lax.psum(
            rounded.astype(jnp.float32).reshape(slots_all, width).astype(jnp.bfloat16),
            ("fsdp", "tensor"),
        ).astype(jnp.float32)
        own_rows = lax.dynamic_slice_in_dim(summed_all, group_index * my_rows, my_rows, 0)
        returned = lax.all_to_all(
            own_rows.reshape(my_rows // E, owned_experts, groups, width).astype(jnp.bfloat16),
            "expert",
            split_axis=2,
            concat_axis=1,
            tiled=True,
        ).astype(jnp.float32)
        back_rows = returned.reshape(my_rows, width)
        local_slot = slot_index - group_index * my_rows
        matches = (local_slot[:, None] == jnp.arange(my_rows)[None, :]).astype(
            jnp.float32
        ) * weights[:, None]
        mixing = jnp.sum(matches.reshape(token_count, 2, my_rows), axis=1)
        token_part = jnp.dot(
            mixing, back_rows, precision=lax.Precision.HIGHEST, preferred_element_type=jnp.float32
        )
        summed = lax.psum_scatter(
            token_part.astype(jnp.bfloat16), ("fsdp", "tensor"), scatter_dimension=1, tiled=True
        )
        outputs.append(summed)
    return (jnp.stack(outputs), first_new, second_new)


def solution(mesh):
    return jax.shard_map(
        on_device,
        mesh=mesh,
        in_specs=(
            P(None, "expert", None),
            P(None, "expert", None),
            P(None, "expert", None),
            P("expert", None, None, ("fsdp", "tensor")),
            P("expert", ("fsdp", "tensor"), None),
            P(None, ("fsdp", "tensor"), "expert"),
            P(None, ("fsdp", "tensor"), "expert"),
            P(None, ("fsdp", "tensor"), "expert"),
            P(None, ("fsdp", "tensor"), None),
            P(None, ("fsdp", "tensor")),
        ),
        out_specs=(
            P(None, "expert", ("fsdp", "tensor")),
            P(None, ("fsdp", "tensor"), "expert"),
            P(None, ("fsdp", "tensor"), "expert"),
        ),
        check_vma=False,
    )
```

profile of v0, /device:TPU:1, one launch (start us, length us, event | category | flops | bytes accessed | tf_op | source)
XLA Modules:
  0.0 471.5 jit_solution(10701331030025720263)
XLA Ops:
  7.2 3.7 negate_convert_fusion
  10.9 9.1 %all-to-all-start = ((bf16[8,64,512]{2,1,0:T(8,128)(2,1)}), bf16[8,64,512]{2,1,0:T(8,128)(2,1)S(1)}, u32[]{:S(2)}, u32[]{:S(2)}) async-start(bf16[8,64,512]{2,1,0:T(8,128)(2,1)} %get-tuple-element.7), calls=%async_computation | async-start | bytes 1048576 | tf_op jit(solution)/shard_map/all_to_all | solution.py:56
  22.1 0.7 fusion.2
  22.8 2.4 copy.112
  25.2 12.8 %all-to-all-done = bf16[8,64,512]{2,1,0:T(8,128)(2,1)S(1)} async-done(((bf16[8,64,512]{2,1,0:T(8,128)(2,1)}), bf16[8,64,512]{2,1,0:T(8,128)(2,1)S(1)}, u32[]{:S(2)}, u32[]{:S(2)}) %all-to-all-start) | async-done | bytes 524320 | tf_op jit(solution)/shard_map/all_to_all | solution.py:56
  38.0 3.6 all-to-all-start.3
  41.6 1.8 fusion
  43.4 2.5 copy.105
  45.9 43.7 %all-to-all-done.3 = bf16[32,8,1,4096]{3,0,2,1:T(8,128)(2,1)S(1)} async-done(((bf16[32,8,1,4096]{3,0,2,1:T(8,128)(2,1)}), bf16[32,8,1,4096]{3,0,2,1:T(8,128)(2,1)S(1)}, u32[]{:S(2)}, u32[]{:S(2)}) %all-to-all-start.3) | async-done | bytes 2097184 | tf_op jit(solution)/shard_map/all_to_all | solution.py:85
  89.7 5.0 %all-to-all-start.1 = ((bf16[32,8,1,4096]{3,0,2,1:T(8,128)(2,1)}), bf16[32,8,1,4096]{3,0,2,1:T(8,128)(2,1)}, u32[]{:S(2)}, u32[]{:S(2)}) async-start(bf16[32,8,1,4096]{3,0,2,1:T(8,128)(2,1)} %copy.105), calls=%async_computation.1 | async-start | bytes 4194304 | tf_op jit(solution)/shard_map/all_to_all | solution.py:85
  94.7 0.6 constant_dynamic-slice_fusion
  95.3 0.2 dynamic-slice_reduce_fusion
  95.5 0.7 iota_compare_fusion.7
  96.4 2.7 reshape.328
  99.2 2.6 slice.49
  101.9 1.7 copy.103
  103.6 2.5 reshape.343
  106.1 1.6 fusion.25
  107.8 2.2 pad_maximum_fusion
  110.0 2.1 reshape.341
  112.1 4.3 fusion.17
  116.5 30.0 %all-to-all-done.1 = bf16[32,8,1,4096]{3,0,2,1:T(8,128)(2,1)} async-done(((bf16[32,8,1,4096]{3,0,2,1:T(8,128)(2,1)}), bf16[32,8,1,4096]{3,0,2,1:T(8,128)(2,1)}, u32[]{:S(2)}, u32[]{:S(2)}) %all-to-all-start.1) | async-done | bytes 2097184 | tf_op jit(solution)/shard_map/all_to_all | solution.py:85
  146.5 4.3 fusion.12
  150.9 0.7 fusion.3
  151.6 0.7 fusion.1
  152.3 2.5 copy.154
  154.8 2.5 copy.153
  157.3 118.7 %all-reduce.3.cloned.1.call-done = (bf16[256,4096]{1,0:T(8,128)(2,1)}, bf16[256,4096]{1,0:T(8,128)(2,1)}) async-done(((bf16[256,4096]{1,0:T(8,128)(2,1)}, bf16[256,4096]{1,0:T(8,128)(2,1)}), (bf16[256,4096]{1,0:T(8,128)(2,1)}, bf16[256,4096]{1,0:T(8,128)(2,1)})) %all-reduce.3.cloned.1.call-update) | async-done | bytes 4194320 | tf_op jit(solution)/shard_map/psum | solution.py:99
  276.1 0.8 fusion.36
  277.0 0.5 broadcast.169
  277.5 1.0 reduce.4
  278.6 0.7 reshape.352
  279.2 6.7 %all-to-all-start.2 = ((bf16[8,2,2048]{2,1,0:T(2,128)(2,1)}), bf16[8,2,2048]{2,1,0:T(2,128)(2,1)S(1)}, u32[]{:S(2)}, u32[]{:S(2)}) async-start(bf16[8,2,2048]{2,1,0:T(2,128)(2,1)} %reshape.352), calls=%async_computation.2 | async-start | bytes 131072 | tf_op jit(solution)/shard_map/all_to_all | solution.py:104
  286.0 7.1 %all-to-all-done.2 = bf16[8,2,2048]{2,1,0:T(2,128)(2,1)S(1)} async-done(((bf16[8,2,2048]{2,1,0:T(2,128)(2,1)}), bf16[8,2,2048]{2,1,0:T(2,128)(2,1)S(1)}, u32[]{:S(2)}, u32[]{:S(2)}) %all-to-all-start.2) | async-done | bytes 65568 | tf_op jit(solution)/shard_map/all_to_all | solution.py:104
  293.2 0.6 convolution_convert_fusion.5
  293.9 1.3 copy.119
  295.2 0.9 fusion.37
  296.2 1.0 reduce.3
  297.2 0.7 reshape.350
  297.8 3.3 all-to-all-start.4
  301.3 7.1 %all-to-all-done.4 = bf16[8,2,2048]{2,1,0:T(2,128)(2,1)S(1)} async-done(((bf16[8,2,2048]{2,1,0:T(2,128)(2,1)}), bf16[8,2,2048]{2,1,0:T(2,128)(2,1)S(1)}, u32[]{:S(2)}, u32[]{:S(2)}) %all-to-all-start.4) | async-done | bytes 65568 | tf_op jit(solution)/shard_map/all_to_all | solution.py:104
  308.4 0.6 convolution_convert_fusion.4
  309.0 1.3 copy.121
  310.4 64.3 %reduce-scatter.7.cloned.1.call-done = bf16[128,64]{1,0:T(8,128)(2,1)} async-done(((bf16[4096,64]{1,0:T(8,128)(2,1)}), bf16[128,64]{1,0:T(8,128)(2,1)}) %reduce-scatter.7.cloned.1.call-update) | async-done | bytes 16400
  374.7 0.8 copy.120
  375.5 88.0 %reduce-scatter.9.cloned.1.call-done = bf16[128,64]{1,0:T(8,128)(2,1)} async-done(((bf16[4096,64]{1,0:T(8,128)(2,1)}), bf16[128,64]{1,0:T(8,128)(2,1)}) %reduce-scatter.9.cloned.1.call-update) | async-done | bytes 16400
  463.5 0.8 copy.122
  464.3 0.6 pad_maximum_fusion.1
  (54 shorter events, 3.0 us)
Async XLA Ops:
  7.2 88.2 %copy-start = (s32[8,1,4]{0,2,1:T(4,128)S(1)}, s32[8,1,4]{0,2,1:T(4,128)}, u32[]{:S(2)}) copy-start(s32[8,1,4]{0,2,1:T(4,128)} %param.18) | copy-start | bytes 388
  7.2 12.9 %copy-start.5 = (s32[2,64,2]{1,2,0:T(2,128)S(1)}, s32[2,64,2]{1,2,0:T(2,128)}, u32[]{:S(2)}) copy-start(s32[2,64,2]{1,2,0:T(2,128)} %param.11) | copy-start | bytes 3076
  10.9 11.1 %copy-start.4 = (bf16[2,64,4096]{2,1,0:T(8,128)(2,1)S(1)}, bf16[2,64,4096]{2,1,0:T(8,128)(2,1)}, u32[]{:S(2)}) copy-start(bf16[2,64,4096]{2,1,0:T(8,128)(2,1)} %param.10) | copy-start | bytes 3145732
  10.9 27.1 %all-to-all-start = ((bf16[8,64,512]{2,1,0:T(8,128)(2,1)}), bf16[8,64,512]{2,1,0:T(8,128)(2,1)S(1)}, u32[]{:S(2)}, u32[]{:S(2)}) async-start(bf16[8,64,512]{2,1,0:T(8,128)(2,1)} %get-tuple-element.7), calls=%async_computation | async-start | bytes 1048576 | tf_op jit(solution)/shard_map/all_to_all | solution.py:56
  38.0 51.6 %all-to-all-start.3 = ((bf16[32,8,1,4096]{3,0,2,1:T(8,128)(2,1)}), bf16[32,8,1,4096]{3,0,2,1:T(8,128)(2,1)S(1)}, u32[]{:S(2)}, u32[]{:S(2)}) async-start(bf16[32,8,1,4096]{3,0,2,1:T(8,128)(2,1)} %copy.112), calls=%async_computation.3 | async-start | bytes 4194304 | tf_op jit(solution)/shard_map/all_to_all | solution.py:85
  45.9 48.8 %copy-start.7 = (s32[8,1]{0,1:T(1,128)S(1)}, s32[8,1]{0,1:T(1,128)}, u32[]{:S(2)}) copy-start(s32[8,1]{0,1:T(1,128)} %param.19) | copy-start | bytes 100
  89.7 6.7 %copy-start.2 = (bf16[32,8,1,4096]{3,0,2,1:T(8,128)(2,1)}, bf16[32,8,1,4096]{3,0,2,1:T(8,128)(2,1)S(1)}, u32[]{:S(2)}) copy-start(bf16[32,8,1,4096]{3,0,2,1:T(8,128)(2,1)S(1)} %all-to-all-done.3) | copy-start | bytes 6291460
  89.7 56.8 %all-to-all-start.1 = ((bf16[32,8,1,4096]{3,0,2,1:T(8,128)(2,1)}), bf16[32,8,1,4096]{3,0,2,1:T(8,128)(2,1)}, u32[]{:S(2)}, u32[]{:S(2)}) async-start(bf16[32,8,1,4096]{3,0,2,1:T(8,128)(2,1)} %copy.105), calls=%async_computation.1 | async-start | bytes 4194304 | tf_op jit(solution)/shard_map/all_to_all | solution.py:85
  94.7 181.4 %all-reduce.3.cloned.1.call-start = ((), (), s32[]{:S(2)}) async-start(), calls=%async_computation.9 | async-start | bytes 8388608 | tf_op jit(solution)/shard_map/psum | solution.py:99
  106.1 1.7 copy-start.1
  116.5 34.4 %copy-start.3 = (bf16[256,4096,1]{1,0,2:T(8,128)(2,1)S(1)}, bf16[256,4096,1]{1,0,2:T(8,128)(2,1)}, u32[]{:S(2)}) copy-start(bf16[256,4096,1]{1,0,2:T(8,128)(2,1)} %reshape.341) | copy-start | bytes 6291460
  157.3 128.7 %copy-start.6 = (f32[2,64,2]{1,2,0:T(2,128)S(1)}, f32[2,64,2]{1,2,0:T(2,128)}, u32[]{:S(2)}) copy-start(f32[2,64,2]{1,2,0:T(2,128)} %param.12) | copy-start | bytes 3076
  279.2 14.0 %all-to-all-start.2 = ((bf16[8,2,2048]{2,1,0:T(2,128)(2,1)}), bf16[8,2,2048]{2,1,0:T(2,128)(2,1)S(1)}, u32[]{:S(2)}, u32[]{:S(2)}) async-start(bf16[8,2,2048]{2,1,0:T(2,128)(2,1)} %reshape.352), calls=%async_computation.2 | async-start | bytes 131072 | tf_op jit(solution)/shard_map/all_to_all | solution.py:104
  285.9 88.7 %reduce-scatter.7.cloned.1.call-start = ((), (), s32[]{:S(2)}) async-start(), calls=%async_computation.7 | async-start | bytes 1081344
  297.8 10.5 %all-to-all-start.4 = ((bf16[8,2,2048]{2,1,0:T(2,128)(2,1)}), bf16[8,2,2048]{2,1,0:T(2,128)(2,1)S(1)}, u32[]{:S(2)}, u32[]{:S(2)}) async-start(bf16[8,2,2048]{2,1,0:T(2,128)(2,1)} %reshape.350), calls=%async_computation.4 | async-start | bytes 131072 | tf_op jit(solution)/shard_map/all_to_all | solution.py:104
  301.2 162.3 %reduce-scatter.9.cloned.1.call-start = ((), (), s32[]{:S(2)}) async-start(), calls=%async_computation.8 | async-start | bytes 1081344
Sparse Core Ops, SparseCore 0:
  157.5 118.5 all-reduce.2
  295.3 79.2 reduce-scatter.6
  378.9 84.5 reduce-scatter.8
where the time goes:
time: 473 us; the launch traced here: 471 us
  waiting for transfers between devices  372 us (79%)
  local copies, waits for them, and re-layouts  29.9 us (6%)
  starting transfers between devices  28 us (6%)
  between operations  14.1 us (3%)
  other arithmetic  14 us (3%)
  matrix products  13.8 us (3%)
    unnamed x5, waiting for transfers between devices  152 us
    psum x1, waiting for transfers between devices, on_device(): lax.psum(rounded.astype(jnp.float32).reshape(slots_all, width).astype(jnp...  119 us
    all_to_all x2, waiting for transfers between devices, on_device(): lax.all_to_all(outgoing, 'expert', split_axis=1, concat_axis=2, tiled=True)  73.7 us
    all_to_all x2, waiting for transfers between devices, on_device(): lax.all_to_all(own_rows.reshape(my_rows // E, owned_experts, groups, widt...  14.2 us
    all_to_all x1, waiting for transfers between devices, on_device(): lax.all_to_all(delta, 'expert', split_axis=0, concat_axis=2, tiled=True)  12.8 us
    all_to_all x2, starting transfers between devices, on_device(): lax.all_to_all(own_rows.reshape(my_rows // E, owned_experts, groups, widt...  10.1 us
  transfers between devices with their start and end apart: 8, of which 8 were waited for; matrix products, arithmetic and copies ran while one was open for 8% of the time, Pallas kernels for 0%

commit v1 on v0

v1 whole, which is shorter than its diff:
```python
import jax
import jax.numpy as jnp
from jax import lax
from jax.experimental import pallas as pl
from jax.experimental.pallas import tpu as pltpu
from jax.sharding import PartitionSpec as P

F32 = jnp.float32
BF16 = jnp.bfloat16
MESH_ID = pl.DeviceIdType.MESH

E = 8
BLOCK_ROWS = 8
MAXCH = 4
CAP = 32
TOK = 64
D = 4096
HS = 256
SLOTS = E * CAP
QUART = 512
LANE = 128
KDOWN = 2 * HS + 128
PIECE = 128

BETA_ONE = 0.9
BETA_TWO = 0.95
LEARN_RATE = 0.03
ADAM_EPS = 1e-08
FIRST_FIX = 1.0 - 0.9**10
SECOND_FIX = 1.0 - 0.95**10


def adam_kernel(list_ref, m_ref, v_ref, g_ref, first_ref, second_ref, delta_ref):
    e = pl.program_id(0)
    grad = g_ref[0].astype(F32)
    first_ref[0] = BETA_ONE * m_ref[0] + (1.0 - BETA_ONE) * grad
    second_ref[0] = BETA_TWO * v_ref[0] + (1.0 - BETA_TWO) * grad * grad
    parts = []
    for j in range(MAXCH):
        rows = pl.ds(pl.multiple_of(list_ref[j, e] * BLOCK_ROWS, BLOCK_ROWS), BLOCK_ROWS)
        top = first_ref[0, rows, :] / FIRST_FIX
        parts.append(
            -(LEARN_RATE * top / (jnp.sqrt(second_ref[0, rows, :] / SECOND_FIX) + ADAM_EPS))
        )
    delta_ref[0] = jnp.concatenate(parts, axis=0).astype(BF16)


def adam(block_list, adam_first, adam_second, gradient):
    rows, cols = adam_first.shape[1:]
    spec = pl.BlockSpec((1, rows, cols), lambda e: (e, 0, 0))
    return pl.pallas_call(
        adam_kernel,
        grid=(E,),
        in_specs=[pl.BlockSpec(memory_space=pltpu.SMEM), spec, spec, spec],
        out_specs=[
            spec,
            spec,
            pl.BlockSpec((1, MAXCH * BLOCK_ROWS, cols), lambda e: (e, 0, 0)),
        ],
        out_shape=[
            jax.ShapeDtypeStruct((E, rows, cols), F32),
            jax.ShapeDtypeStruct((E, rows, cols), F32),
            jax.ShapeDtypeStruct((E, MAXCH * BLOCK_ROWS, cols), BF16),
        ],
        name="adam",
    )(block_list, adam_first, adam_second, gradient)


def tri(j):
    return lax.rem(j * (j + 1) // 2, 4)


def expert_kernel(
    route_ref,
    weight_ref,
    list_ref,
    count_ref,
    tokens,
    gate_up,
    down,
    delta,
    out_ref,
    tok,
    zsend,
    xbuf,
    gu,
    dn,
    acc,
    hid,
    mix,
    tgt,
    r1send,
    r1recv,
    r1own,
    r2send,
    r2recv,
    r2own,
    r3buf,
    back,
    load_sem,
    gu_sem,
    sib_send,
    sib_recv,
    z_send,
    z_recv,
    f_send,
    f_recv,
    d_send,
    d_recv,
    m_send,
    m_recv,
    r1s,
    r1r,
    r2s,
    r2r,
    r3s,
    r3r,
):
    x = lax.axis_index("fsdp")
    z = lax.axis_index("expert")
    t = lax.axis_index("tensor")
    y = t // 2
    c = lax.rem(t, 2)

    def at(i, j, k, core):
        return (lax.rem(x + i, 4), lax.rem(z + k, 8), lax.rem(y + j, 4) * 2 + core)

    def remote(src, dst, ssem, rsem, where):
        return pltpu.make_async_remote_copy(
            src_ref=src,
            dst_ref=dst,
            send_sem=ssem,
            recv_sem=rsem,
            device_id=where,
            device_id_type=MESH_ID,
        )

    barrier = pltpu.get_barrier_semaphore()
    sibling = at(0, 0, 0, 1 - c)
    for i in range(1, 4):
        for where in (at(i, 0, 0, c), at(0, i, 0, c)):
            pl.semaphore_signal(barrier, inc=1, device_id=where, device_id_type=MESH_ID)
    for k in range(8):
        pl.semaphore_signal(
            barrier, inc=1, device_id=at(0, 0, k, 1 - c), device_id_type=MESH_ID
        )
        if k:
            pl.semaphore_signal(
                barrier, inc=1, device_id=at(0, 0, k, c), device_id_type=MESH_ID
            )

    tok_loads = [
        pltpu.make_async_copy(
            tokens.at[c, :, pl.ds(pl.multiple_of(col, QUART), QUART)], tok.at[h], load_sem.at[h]
        )
        for h, col in enumerate((x * QUART, 2048 + y * QUART))
    ]
    for cp in tok_loads:
        cp.start()

    def chunk_rows(h, i):
        own = x + h * (y - x)
        start = h * 2048 + lax.rem(own - i + 4, 4) * QUART
        return pl.ds(pl.multiple_of(start, QUART), QUART)

    def gu_load(q):
        rows = chunk_rows(lax.rem(q, 2), tri(q // 2))
        return pltpu.make_async_copy(
            gate_up.at[:, rows, :], gu.at[0, :, rows, :], gu_sem.at[q]
        )

    @pl.loop(0, 8)
    def _(q):
        gu_load(q).start()

    down_load = pltpu.make_async_copy(down, dn.at[pl.ds(0, HS)], load_sem.at[2])
    down_load.start()
    delta_cols = pl.ds(pl.multiple_of(z * QUART, QUART), QUART)
    delta_load = pltpu.make_async_copy(
        delta.at[z], dn.at[pl.ds(2 * HS, CAP), delta_cols], load_sem.at[3]
    )
    delta_load.start()

    lower = (
        lax.broadcasted_iota(jnp.int32, (TOK, TOK), 0)
        < lax.broadcasted_iota(jnp.int32, (TOK, TOK), 1)
    ).astype(BF16)
    expert_ids = lax.broadcasted_iota(jnp.int32, (E, TOK), 0)
    slot_ids = lax.broadcasted_iota(jnp.int32, (CAP, TOK), 0).astype(F32)

    def slots_of(step):
        named = route_ref[step]
        hits = [named[k : k + 1, :] == expert_ids for k in range(2)]
        any_hit = jnp.where(hits[0] | hits[1], 1.0, 0.0)
        place = jnp.dot(any_hit.astype(BF16), lower, preferred_element_type=F32)
        place = jnp.where(any_hit > 0.5, place, -1.0)
        return hits, [slot_ids == place[e : e + 1, :] for e in range(E)]

    _, chosen = slots_of(c)
    selector = jnp.concatenate([jnp.where(m, 1.0, 0.0) for m in chosen], axis=0).astype(BF16)
    for h in range(2):
        tok_loads[h].wait()
        zsend[h] = jnp.dot(selector, tok[h], preferred_element_type=F32).astype(BF16)
    own_rows = pl.ds(pl.multiple_of(z * CAP, CAP), CAP)
    for h in range(2):
        xbuf[h, 0, own_rows, :] = zsend[h, own_rows, :]

    pl.semaphore_wait(barrier, 21)

    def z_copy(h, k):
        e = lax.rem(z + k, 8)
        rows = pl.ds(pl.multiple_of(e * CAP, CAP), CAP)
        return remote(
            zsend.at[h, rows, :],
            xbuf.at[h, 0, own_rows, :],
            z_send.at[h, k],
            z_recv.at[h, k],
            at(0, 0, k, c),
        )

    for k in (4, 3, 5, 2, 6, 1, 7):
        for h in range(2):
            z_copy(h, k).start()

    def forward(h, i, k):
        rows = pl.ds(pl.multiple_of(lax.rem(z - k + 8, 8) * CAP, CAP), CAP)
        return remote(
            xbuf.at[h, 0, rows, :],
            xbuf.at[h, i, rows, :],
            f_send.at[h, i],
            f_recv.at[h, i],
            at(i * (1 - h), i * h, 0, c),
        )

    def forward_all(h, i):
        return remote(
            xbuf.at[h, 0],
            xbuf.at[h, i],
            f_send.at[h, i],
            f_recv.at[h, i],
            at(i * (1 - h), i * h, 0, c),
        )

    for i in (2, 1, 3):
        for h in range(2):
            forward(h, i, 0).start()

    def gu_swap(q):
        rows = chunk_rows(lax.rem(q, 2), tri(q // 2))
        return remote(
            gate_up.at[:, rows, :],
            gu.at[1, :, rows, :],
            sib_send.at[q],
            sib_recv.at[q],
            sibling,
        )

    @pl.loop(0, 8)
    def _(q):
        gu_swap(q).start()

    def d_copy(k):
        e = lax.rem(z + k, 8)
        return remote(
            delta.at[e],
            dn.at[pl.ds(2 * HS, CAP), delta_cols],
            d_send.at[k],
            d_recv.at[k],
            at(0, 0, k, c),
        )

    for k in (4, 3, 5, 2, 6, 1, 7):
        d_copy(k).start()

    down_swap = remote(
        down, dn.at[pl.ds(HS, HS)], m_send.at[0], m_recv.at[0], sibling
    )
    down_swap.start()

    here = lax.broadcasted_iota(jnp.int32, (MAXCH, E), 1) == z
    blocks = jnp.sum(jnp.where(here, list_ref[...], 0), axis=1, keepdims=True)
    count = jnp.sum(jnp.where(here[0:1], count_ref[...], 0), axis=1, keepdims=True)
    lane = lax.broadcasted_iota(jnp.int32, (8, LANE), 1)

    def targets(first_lane, first_unit):
        units = jnp.full((8, LANE), -1, jnp.int32)
        for j in range(MAXCH):
            start = first_lane + BLOCK_ROWS * j
            live = (lane >= start) & (lane < start + BLOCK_ROWS) & (count > j)
            unit = first_unit + 4 * (BLOCK_ROWS * blocks[j : j + 1, :] + lane - start)
            units = jnp.where(live, unit, units)
        return units.astype(F32)

    tgt[0] = targets(0, 0)
    tgt[1] = targets(CAP, HS)
    target_swap = remote(tgt.at[1], tgt.at[2], m_send.at[1], m_recv.at[1], sibling)
    target_swap.start()
    dn[pl.ds(2 * HS + 2 * CAP, 2 * CAP), :] = jnp.zeros((2 * CAP, D), BF16)

    for k in (1, 7, 2, 6, 3, 5, 4):
        for h in range(2):
            z_copy(h, k).wait_recv()
            for i in (2, 1, 3):
                forward(h, i, k).start()

    for step in range(2):
        hits, chosen = slots_of(step)
        w = weight_ref[step]
        by_expert = jnp.where(hits[0], w[0:1, :], 0.0) + jnp.where(hits[1], w[1:2, :], 0.0)
        full = jnp.concatenate(
            [jnp.where(chosen[e], by_expert[e : e + 1, :], 0.0) for e in range(E)], axis=0
        )
        full = full.T
        high = full.astype(BF16)
        mix[step, pl.ds(0, TOK), :] = high
        mix[step, pl.ds(TOK, TOK), :] = (full - high.astype(F32)).astype(BF16)

    def project(q, first):
        h, i = lax.rem(q, 2), tri(q // 2)
        gu_load(q).wait()
        gu_swap(q).wait_recv()
        rows = chunk_rows(h, i)
        block = xbuf[h, i]
        for s in range(2):
            for g in range(2):
                term = jnp.dot(block, gu[s, g, rows, :], preferred_element_type=F32)
                if first:
                    acc[2 * s + g] = term
                else:
                    acc[2 * s + g] += term

    project(0, True)

    @pl.loop(1, 2)
    def _(q):
        project(q, False)

    @pl.loop(2, 8)
    def _(q):
        forward_all(lax.rem(q, 2), tri(q // 2)).wait_recv()
        project(q, False)

    delta_load.wait()
    for k in range(1, 8):
        d_copy(k).wait_recv()
    delta_swap = remote(
        dn.at[pl.ds(2 * HS, CAP)],
        dn.at[pl.ds(2 * HS + CAP, CAP)],
        m_send.at[2],
        m_recv.at[2],
        sibling,
    )
    delta_swap.start()

    for s in range(2):
        gate = acc[2 * s]
        hid[:, pl.ds(s * HS, HS)] = (jax.nn.silu(gate) * acc[2 * s + 1]).astype(BF16)
    target_swap.wait_recv()
    unit = jnp.where(lane < CAP, tgt[0], tgt[2])[0:1, :]
    picks = (
        lax.broadcasted_iota(jnp.int32, (2 * HS, LANE), 0).astype(F32) == unit
    ).astype(BF16)
    hid[:, pl.ds(2 * HS, LANE)] = jnp.dot(
        hid[:, pl.ds(0, 2 * HS)], picks, preferred_element_type=F32
    ).astype(BF16)

    down_load.wait()
    down_swap.wait_recv()
    delta_swap.wait_recv()

    def down_term(h, i):
        cols = []
        for j in range(4):
            a, b = i + h * (j - i), j + h * (i - j)
            block = 8 * lax.rem(x + a, 4) + 2 * lax.rem(y + b, 4) + h
            cols.append(dn[:, pl.ds(pl.multiple_of(block * LANE, LANE), LANE)])
        return jnp.dot(hid[...], jnp.concatenate(cols, axis=1), preferred_element_type=F32)

    def r1_copy(h, i, p):
        rows = pl.ds(p * PIECE, PIECE)
        return remote(
            r1send.at[h, i - 1, rows, :],
            r1recv.at[h, i - 1, rows, :],
            r1s.at[h, i - 1, p],
            r1r.at[h, i - 1, p],
            at(i * (1 - h), i * h, 0, c),
        )

    @pl.loop(0, 6)
    def _(q):
        h, i = lax.rem(q, 2), lax.rem(6 - tri(q // 2), 4)
        r1send[h, i - 1] = down_term(h, i).astype(BF16)
        for p in range(2):
            r1_copy(h, i, p).start()

    @pl.loop(0, 2)
    def _(h):
        r1own[h] = down_term(h, 0)

    def r2_copy(h, j, p):
        rows = pl.ds(p * PIECE, PIECE)
        return remote(
            r2send.at[h, j - 1, rows, :],
            r2recv.at[h, j - 1, rows, :],
            r2s.at[h, j - 1, p],
            r2r.at[h, j - 1, p],
            at(j * h, j * (1 - h), 0, c),
        )

    for p in range(2):
        rows = pl.ds(p * PIECE, PIECE)
        for h in range(2):
            for i in (1, 3, 2):
                r1_copy(h, i, p).wait_recv()
            for j in (2, 1, 3, 0):
                cols = pl.ds(j * LANE, LANE)
                total = r1own[h, rows, cols]
                for i in range(3):
                    total += r1recv[h, i, rows, cols].astype(F32)
                if j:
                    r2send[h, j - 1, rows, :] = total.astype(BF16)
                    r2_copy(h, j, p).start()
                else:
                    r2own[h, rows, :] = total

    def r3_copy(h, e):
        rows = pl.ds(pl.multiple_of(e * CAP, CAP), CAP)
        return remote(
            r3buf.at[h, rows, :],
            back.at[c, own_rows, :],
            r3s.at[e, h],
            r3r.at[z, c],
            (x, e, y * 2 + h),
        )

    def r3_wait(step, e):
        rows = pl.ds(pl.multiple_of(e * CAP, CAP), CAP)
        remote(
            r3buf.at[step, rows, :],
            back.at[step, rows, :],
            r3s.at[e, step],
            r3r.at[e, step],
            (x, e, y * 2 + step),
        ).wait_recv()

    def not_self(e, core):
        return jnp.logical_or(e != z, core != c)

    for p in range(2):
        rows = pl.ds(p * PIECE, PIECE)
        for h in range(2):
            for j in (1, 3, 2):
                r2_copy(h, j, p).wait_recv()
            total = r2own[h, rows, :]
            for j in range(3):
                total += r2recv[h, j, rows, :].astype(F32)
            r3buf[h, rows, :] = total.astype(BF16)
            for e in range(4 * p, 4 * p + 4):

                @pl.when(not_self(e, h))
                def _(h=h, e=e):
                    r3_copy(h, e).start()

    back[c, own_rows, :] = r3buf[c, own_rows, :]
    for step in range(2):
        for e in range(E):

            @pl.when(not_self(e, step))
            def _(step=step, e=e):
                r3_wait(step, e)

        both = jnp.dot(mix[step], back[step], preferred_element_type=F32)
        out_ref[step] = (both[:TOK] + both[TOK:]).astype(BF16)

    for h in range(2):
        for k in range(1, 8):
            z_copy(h, k).wait_send()
        for i in range(1, 4):
            forward_all(h, i).wait_send()
            for p in range(2):
                r1_copy(h, i, p).wait_send()
                r2_copy(h, i, p).wait_send()
        for e in range(E):

            @pl.when(not_self(e, h))
            def _(h=h, e=e):
                r3_copy(h, e).wait_send()

    @pl.loop(0, 8)
    def _(q):
        gu_swap(q).wait_send()

    for k in range(1, 8):
        d_copy(k).wait_send()
    for cp in (down_swap, target_swap, delta_swap):
        cp.wait_send()


def expert_layer(route, weight, block_list, block_count, tokens, gate_up, down, delta):
    vmem = pl.BlockSpec(memory_space=pltpu.VMEM)
    hbm = pl.BlockSpec(memory_space=pl.ANY)
    dma = pltpu.SemaphoreType.DMA
    return pl.pallas_call(
        expert_kernel,
        in_specs=[vmem] * 4 + [hbm] * 4,
        out_specs=vmem,
        out_shape=jax.ShapeDtypeStruct((2, TOK, LANE), BF16),
        scratch_shapes=[
            pltpu.VMEM((2, TOK, QUART), BF16),
            pltpu.VMEM((2, SLOTS, QUART), BF16),
            pltpu.VMEM((2, 4, SLOTS, QUART), BF16),
            pltpu.VMEM((2, 2, D, HS), BF16),
            pltpu.VMEM((KDOWN, D), BF16),
            pltpu.VMEM((4, SLOTS, HS), F32),
            pltpu.VMEM((SLOTS, KDOWN), BF16),
            pltpu.VMEM((2, 2 * TOK, SLOTS), BF16),
            pltpu.VMEM((3, 8, LANE), F32),
            pltpu.VMEM((2, 3, SLOTS, QUART), BF16),
            pltpu.VMEM((2, 3, SLOTS, QUART), BF16),
            pltpu.VMEM((2, SLOTS, QUART), F32),
            pltpu.VMEM((2, 3, SLOTS, LANE), BF16),
            pltpu.VMEM((2, 3, SLOTS, LANE), BF16),
            pltpu.VMEM((2, SLOTS, LANE), F32),
            pltpu.VMEM((2, SLOTS, LANE), BF16),
            pltpu.VMEM((2, SLOTS, LANE), BF16),
            dma((4,)),
            dma((8,)),
            dma((8,)),
            dma((8,)),
            dma((2, 8)),
            dma((2, 8)),
            dma((2, 4)),
            dma((2, 4)),
            dma((8,)),
            dma((8,)),
            dma((3,)),
            dma((3,)),
            dma((2, 3, 2)),
            dma((2, 3, 2)),
            dma((2, 3, 2)),
            dma((2, 3, 2)),
            dma((8, 2)),
            dma((8, 2)),
        ],
        compiler_params=pltpu.CompilerParams(
            collective_id=1, has_side_effects=True, vmem_limit_bytes=48 * 2**20
        ),
        cost_estimate=pl.CostEstimate(
            flops=3_600_000_000, bytes_accessed=8_000_000, transcendentals=131072
        ),
        name="experts",
    )(route, weight, block_list, block_count, tokens, gate_up, down, delta)


def on_device(
    tokens,
    route,
    route_weight,
    gate_up,
    down_weight,
    adam_first,
    adam_second,
    gradient,
    block_list,
    block_count,
):
    lists = block_list[:, 0, :].T
    first_new, second_new, delta = adam(lists, adam_first, adam_second, gradient)
    mixed = expert_layer(
        route.transpose(0, 2, 1),
        route_weight.transpose(0, 2, 1),
        lists,
        block_count.T,
        tokens,
        gate_up[0],
        down_weight[0],
        delta,
    )
    return mixed, first_new, second_new


def solution(mesh):
    return jax.shard_map(
        on_device,
        mesh=mesh,
        in_specs=(
            P(None, "expert", None),
            P(None, "expert", None),
            P(None, "expert", None),
            P("expert", None, None, ("fsdp", "tensor")),
            P("expert", ("fsdp", "tensor"), None),
            P(None, ("fsdp", "tensor"), "expert"),
            P(None, ("fsdp", "tensor"), "expert"),
            P(None, ("fsdp", "tensor"), "expert"),
            P(None, ("fsdp", "tensor"), None),
            P(None, ("fsdp", "tensor")),
        ),
        out_specs=(
            P(None, "expert", ("fsdp", "tensor")),
            P(None, ("fsdp", "tensor"), "expert"),
            P(None, ("fsdp", "tensor"), "expert"),
        ),
        check_vma=False,
    )
```

time: 473 us -> 76.6 us (0.16)
  waiting for transfers between devices: 372 us -> 0 us
  Pallas kernels: 0 us -> 68.5 us
  starting transfers between devices: 28 us -> 0 us
  local copies, waits for them, and re-layouts: 29.9 us -> 7.08 us
  other arithmetic: 14 us -> 0 us
  matrix products: 13.8 us -> 0 us
  between operations: 14.1 us -> 0.65 us
    unnamed x5 -> x0, waiting for transfers between devices: 152 us -> none
    psum x1 -> x0, waiting for transfers between devices: 119 us -> none  [on_device(): lax.psum(rounded.astype(jnp.float32).reshape(slots_all, width).astype(jnp...]
    all_to_all x5 -> x0, waiting for transfers between devices: 101 us -> none  [the longest x2 73.7 us: on_device(): lax.all_to_all(outgoing, 'expert', split_axis=1, concat_axis=2, tiled=True)]
    pallas_call x0 -> x2, Pallas kernels: none -> 68.5 us  [the longest x1 62.6 us: expert_layer(): pl.pallas_call(expert_kernel, in_specs=[vmem] * 4 + [hbm] * 4, out_specs=...]
    all_to_all x5 -> x0, starting transfers between devices: 27.8 us -> none  [the longest x2 10.1 us: on_device(): lax.all_to_all(own_rows.reshape(my_rows // E, owned_experts, groups, widt...]
    dot_general x8 -> x0, matrix products: 13.8 us -> none  [the longest x2 8.61 us: on_device(): jnp.einsum('cxed,xgdh->cxegh', slot_block, gate_up, preferred_element_typ...]
    reshape x3 -> x0, local copies, waits for them, and re-layouts: 7.69 us -> none  [the longest x2 4.95 us: on_device(): outgoing = gathered.astype(jnp.bfloat16).reshape(CAP, E, 1, width)]
    convert_element_type x9 -> x0, other arithmetic: 7.53 us -> none  [the longest x1 3.74 us: adam_moments(): return (first_new, second_new, (-step_size).astype(jnp.bfloat16))]
  transfers between devices with their start and end apart: 8 -> 0, of which waited for: 8 -> 0; matrix products, arithmetic and copies ran while one was open for 8% -> 0% of each run, Pallas kernels for 0% -> 0%
where the time goes in v1:
time: 76.6 us; the launch traced here: 76.2 us
  Pallas kernels  68.5 us (89%)
  local copies, waits for them, and re-layouts  7.08 us (9%)
    pallas_call x1, Pallas kernels, expert_layer(): pl.pallas_call(expert_kernel, in_specs=[vmem] * 4 + [hbm] * 4, out_specs=...  62.6 us
    unnamed x15, local copies, waits for them, and re-layouts  7.08 us
    pallas_call x1, Pallas kernels, adam(): pl.pallas_call(adam_kernel, grid=(E,), in_specs=[pl.BlockSpec(memory_spac...  5.89 us

profile of v1, /device:TPU:1, one launch (start us, length us, event | category | flops | bytes accessed | tf_op | source)
XLA Modules:
  0.0 76.2 jit_solution(3663167068047273083)
XLA Ops:
  0.6 5.9 %adam.1 = (f32[8,64,512]{2,1,0:T(8,128)}, f32[8,64,512]{2,1,0:T(8,128)}, bf16[8,32,512]{2,1,0:T(8,128)(2,1)}) custom-call(s32[4,8]{1,0:T(4,128)} %bitcast.8, f32[8,64,512]{2,1,0:T(8,128)} %m_ref.1, f32[8,64,512]{2,1,0:T(8,128)} %v_ref.1, bf16[8,64,512]{2,1,0:T(8,128)(2,1)} %g_ref.1), custom_call_target="tpu_custom_call" | custom-call | tf_op jit(solution)/shard_map/adam/pallas_call | solution.py:51
  6.5 0.0 copy-start
  6.5 0.7 copy-done
  7.2 0.0 copy-start.1
  7.2 1.6 %copy-done.1 = bf16[1,256,4096]{2,1,0:T(8,128)(2,1)S(1)} copy-done((bf16[1,256,4096]{2,1,0:T(8,128)(2,1)S(1)}, bf16[1,256,4096]{2,1,0:T(8,128)(2,1)}, u32[]{:S(2)}) %copy-start.1) | copy-done | bytes 2097176
  8.8 0.0 copy-start.2
  8.8 1.2 %copy-done.2 = bf16[2,64,4096]{2,1,0:T(8,128)(2,1)S(1)} copy-done((bf16[2,64,4096]{2,1,0:T(8,128)(2,1)S(1)}, bf16[2,64,4096]{2,1,0:T(8,128)(2,1)}, u32[]{:S(2)}) %copy-start.2) | copy-done | bytes 1048600
  10.0 0.0 copy-start.3
  10.0 0.9 %copy-done.3 = bf16[8,32,512]{2,1,0:T(8,128)(2,1)S(1)} copy-done((bf16[8,32,512]{2,1,0:T(8,128)(2,1)S(1)}, bf16[8,32,512]{2,1,0:T(8,128)(2,1)}, u32[]{:S(2)}) %copy-start.3) | copy-done | bytes 262168
  11.0 0.0 copy-start.4
  11.0 0.7 copy-done.4
  11.6 0.0 copy-start.5
  11.7 0.7 copy-done.5
  12.3 0.0 copy-start.6
  12.3 0.7 copy-done.6
  13.0 62.6 %experts.1 = bf16[2,64,128]{2,1,0:T(8,128)(2,1)S(1)} custom-call(s32[2,2,64]{2,1,0:T(2,128)S(1)} %bitcast.11, f32[2,2,64]{2,1,0:T(2,128)S(1)} %bitcast.12, s32[4,8]{1,0:T(4,128)S(1)} %bitcast.9, s32[1,8]{1,0:T(1,128)S(1)} %bitcast.13, bf16[2,64,4096]{2,1,0:T(8,128)(2,1)S(1)} %copy-done.2, bf16[2,4096,256]{2,1,0:T(8,128)(2,1)} %bitcast.14, ...), custom_call_target="tpu_custom_call" | custom-call | flops 3600000000 | bytes 8000000 | tf_op jit(solution)/shard_map/experts/pallas_call | solution.py:503
  75.6 0.6 copy.14
Async XLA Ops:
  6.5 0.7 copy-start
  7.2 1.6 %copy-start.1 = (bf16[1,256,4096]{2,1,0:T(8,128)(2,1)S(1)}, bf16[1,256,4096]{2,1,0:T(8,128)(2,1)}, u32[]{:S(2)}) copy-start(bf16[1,256,4096]{2,1,0:T(8,128)(2,1)} %param.14) | copy-start | bytes 6291460
  8.8 1.2 %copy-start.2 = (bf16[2,64,4096]{2,1,0:T(8,128)(2,1)S(1)}, bf16[2,64,4096]{2,1,0:T(8,128)(2,1)}, u32[]{:S(2)}) copy-start(bf16[2,64,4096]{2,1,0:T(8,128)(2,1)} %tokens.1) | copy-start | bytes 3145732
  10.0 0.9 %copy-start.3 = (bf16[8,32,512]{2,1,0:T(8,128)(2,1)S(1)}, bf16[8,32,512]{2,1,0:T(8,128)(2,1)}, u32[]{:S(2)}) copy-start(bf16[8,32,512]{2,1,0:T(8,128)(2,1)} %get-tuple-element.6.delta) | copy-start | bytes 786436
  11.0 0.7 copy-start.4
  11.6 0.7 copy-start.5
  12.3 0.7 copy-start.6

commit v2 on v1

v2 whole, which is shorter than its diff:
```python
import functools

import jax
import jax.numpy as jnp
from jax import lax
from jax.experimental import pallas as pl
from jax.experimental.pallas import tpu as pltpu
from jax.sharding import PartitionSpec as P

F32 = jnp.float32
BF16 = jnp.bfloat16
MESH_ID = pl.DeviceIdType.MESH

E = 8
BLOCK_ROWS = 8
MAXCH = 4
CAP = 32
TOK = 64
D = 4096
HS = 256
SLOTS = E * CAP
QUART = 512
LANE = 128
KDOWN = 2 * HS + 128
NEAR = (0, 1, 7, 2, 6, 3, 5, 4)
HALF = 128
QROWS = 64
LOW = 3
VMEM_BYTES = 60 * 2**20

BETA_ONE = 0.9
BETA_TWO = 0.95
LEARN_RATE = 0.03
ADAM_EPS = 1e-08
FIRST_FIX = 1.0 - 0.9**10
SECOND_FIX = 1.0 - 0.95**10


def moments_kernel(first_part, m_in, v_in, g_in, *refs):
    m_out, v_out, one, two, grad, sems = refs[-6:]

    def loads(e):
        return [
            pltpu.make_async_copy(src.at[e], dst.at[e], sems.at[n, e])
            for n, (src, dst) in enumerate(((m_in, one), (v_in, two), (g_in, grad)))
        ]

    def stores(e):
        return [
            pltpu.make_async_copy(src.at[e], dst.at[e], sems.at[n + 3, e])
            for n, (src, dst) in enumerate(((one, m_out), (two, v_out)))
        ]

    low = lax.axis_index("expert") < LOW

    @pl.when(low if first_part else jnp.logical_not(low))
    def _():
        for e in range(E):
            for cp in loads(e):
                cp.start()
        for e in range(E):
            for cp in loads(e):
                cp.wait()
            wide = grad[e].astype(F32)
            one[e] = BETA_ONE * one[e] + (1.0 - BETA_ONE) * wide
            two[e] = BETA_TWO * two[e] + (1.0 - BETA_TWO) * wide * wide
            for cp in stores(e):
                cp.start()
        for e in range(E):
            for cp in stores(e):
                cp.wait()


def moments(first_part, *arrays):
    hbm = pl.BlockSpec(memory_space=pltpu.HBM)
    like = arrays[0]
    shape = jax.ShapeDtypeStruct(like.shape, F32)
    return pl.pallas_call(
        functools.partial(moments_kernel, first_part),
        in_specs=[hbm] * len(arrays),
        out_specs=[hbm] * 2,
        out_shape=[shape, shape],
        scratch_shapes=[
            pltpu.VMEM(like.shape, F32),
            pltpu.VMEM(like.shape, F32),
            pltpu.VMEM(like.shape, BF16),
            pltpu.SemaphoreType.DMA((5, E)),
        ],
        input_output_aliases={} if first_part else {3: 0, 4: 1},
        compiler_params=pltpu.CompilerParams(vmem_limit_bytes=VMEM_BYTES),
        name="moments_first" if first_part else "moments_last",
    )(*arrays)


def kernel(
    tokens,
    route_in,
    weight_in,
    gate_up,
    down,
    moment_one,
    moment_two,
    gradient,
    list_in,
    count_in,
    mixed,
    route_ref,
    weight_ref,
    list_ref,
    count_ref,
    one,
    two,
    grad,
    delta,
    tok,
    zsend,
    xbuf,
    gu,
    dn,
    acc,
    hid,
    mix,
    tgt,
    picks,
    far,
    via,
    near,
    held,
    came,
    own,
    r2send,
    r2recv,
    r2own,
    r3buf,
    back,
    load_sem,
    gu_sem,
    adam_sem,
    sib_send,
    sib_recv,
    z_send,
    z_recv,
    p_send,
    p_recv,
    f_send,
    f_recv,
    y_send,
    y_recv,
    d_send,
    d_recv,
    m_send,
    m_recv,
    far_s,
    far_r,
    early_s,
    early_r,
    late_s,
    late_r,
    r2s,
    r2r,
    r3s,
    r3r,
):
    x = lax.axis_index("fsdp")
    z = lax.axis_index("expert")
    t = lax.axis_index("tensor")
    y = t // 2
    c = lax.rem(t, 2)

    def at(i, j, k, core):
        return (lax.rem(x + i, 4), lax.rem(z + k, 8), lax.rem(y + j, 4) * 2 + core)

    def along(h, i):
        return at(i * (1 - h), i * h, 0, c)

    def remote(src, dst, ssem, rsem, where):
        return pltpu.make_async_remote_copy(
            src_ref=src,
            dst_ref=dst,
            send_sem=ssem,
            recv_sem=rsem,
            device_id=where,
            device_id_type=MESH_ID,
        )

    barrier = pltpu.get_barrier_semaphore()
    sibling = at(0, 0, 0, 1 - c)
    for i in range(1, 4):
        for h in range(2):
            pl.semaphore_signal(barrier, inc=1, device_id=along(h, i), device_id_type=MESH_ID)
    for k in range(8):
        pl.semaphore_signal(
            barrier, inc=1, device_id=at(0, 0, k, 1 - c), device_id_type=MESH_ID
        )
        if k:
            pl.semaphore_signal(
                barrier, inc=1, device_id=at(0, 0, k, c), device_id_type=MESH_ID
            )

    def small(src, dst, n):
        return pltpu.make_async_copy(src, dst, load_sem.at[n])

    route_load = small(route_in, route_ref, 4)
    columns = pl.ds(pl.multiple_of((4 * x + y) * 2 * LANE, 2 * LANE), 2 * LANE)
    tok_load = small(tokens.at[c, :, columns], tok, 0)
    small_loads = [
        small(list_in, list_ref, 6),
        small(count_in, count_ref, 7),
        small(weight_in, weight_ref, 8),
    ]
    adam_loads = [
        pltpu.make_async_copy(src, dst, adam_sem.at[n])
        for n, (src, dst) in enumerate(((moment_one, one), (moment_two, two), (gradient, grad)))
    ]
    down_load = small(down, dn.at[pl.ds(0, HS)], 2)
    for cp in [route_load, tok_load] + small_loads + adam_loads:
        cp.start()

    def gu_load(q):
        rows = pl.ds(pl.multiple_of(q * QUART, QUART), QUART)
        return pltpu.make_async_copy(
            gate_up.at[:, rows, :], gu.at[0, :, rows, :], gu_sem.at[q]
        )

    lower = (
        lax.broadcasted_iota(jnp.int32, (TOK, TOK), 0)
        < lax.broadcasted_iota(jnp.int32, (TOK, TOK), 1)
    ).astype(BF16)
    expert_ids = lax.broadcasted_iota(jnp.int32, (E, TOK), 0)
    slot_ids = lax.broadcasted_iota(jnp.int32, (CAP, TOK), 0).astype(F32)

    def slots_of(step):
        named = route_ref[step]
        hits = [named[k : k + 1, :] == expert_ids for k in range(2)]
        any_hit = jnp.where(hits[0] | hits[1], 1.0, 0.0)
        place = jnp.dot(any_hit.astype(BF16), lower, preferred_element_type=F32)
        place = jnp.where(any_hit > 0.5, place, -1.0)
        return hits, [slot_ids == place[e : e + 1, :] for e in range(E)]

    route_load.wait()
    _, chosen = slots_of(c)
    selector = jnp.concatenate([jnp.where(m, 1.0, 0.0) for m in chosen], axis=0).astype(BF16)
    tok_load.wait()
    picked = jnp.dot(selector, tok[...], preferred_element_type=F32).astype(BF16)
    for h in range(2):
        zsend[h] = picked[:, h * LANE : (h + 1) * LANE]
    own_rows = pl.ds(pl.multiple_of(z * CAP, CAP), CAP)
    for h in range(2):
        xbuf[h, 0, 0, pl.ds(0, CAP), :] = zsend[h, own_rows, :]

    pl.semaphore_wait(barrier, 21)

    def z_copy(n):
        rows = pl.ds(pl.multiple_of(lax.rem(z + NEAR[n], 8) * CAP, CAP), CAP)
        return remote(
            zsend.at[:, rows, :],
            xbuf.at[:, 0, 0, pl.ds(n * CAP, CAP), :],
            z_send.at[n],
            z_recv.at[n],
            at(0, 0, NEAR[n], c),
        )

    for n in range(1, 8):
        z_copy(n).start()

    def first_copy(h, i, g):
        rows = pl.ds(g * HALF, HALF)
        return remote(
            xbuf.at[h, 0, 0, rows, :],
            xbuf.at[h, 0, i, rows, :],
            p_send.at[h, i, g],
            p_recv.at[h, i, g],
            along(h, i),
        )

    def second_copy(h, w, i, g):
        rows = pl.ds(g * HALF, HALF)
        return remote(
            xbuf.at[h, 0, i, rows, :],
            xbuf.at[h, 1 + 2 * w, i, rows, :],
            f_send.at[h, w, i, g],
            f_recv.at[h, w, i, g],
            along(1 - h, 1 + 2 * w),
        )

    def relay(h, w, i, g):
        rows = pl.ds(g * HALF + w * QROWS, QROWS)
        return remote(
            xbuf.at[h, 1 + 2 * w, i, rows, :],
            xbuf.at[h, 2, i, rows, :],
            y_send.at[h, w, i, g],
            y_recv.at[h, w, i, g],
            along(1 - h, 1 + 2 * w),
        )

    def start_group(g):
        for n in range(4 * g, 4 * g + 4):
            if n:
                z_copy(n).wait_recv()
        for h in range(2):
            for w in range(2):
                first_copy(h, 1 + 2 * w, g).start()
                second_copy(h, w, 0, g).start()
            first_copy(h, 2, g).start()

    def spread(g):
        for i in (1, 3, 2):
            for h in range(2):
                first_copy(h, i, g).wait_recv()
                for w in range(2):
                    second_copy(h, w, i, g).start()

    def pass_on(i, g):
        for h in range(2):
            for w in range(2):
                second_copy(h, w, i, g).wait_recv()
                relay(h, w, i, g).start()

    def gu_swap(q):
        rows = pl.ds(pl.multiple_of(q * QUART, QUART), QUART)
        return remote(
            gate_up.at[:, rows, :],
            gu.at[1, :, rows, :],
            sib_send.at[q],
            sib_recv.at[q],
            sibling,
        )

    @pl.loop(0, 8)
    def _(q):
        gu_load(q).start()
        gu_swap(q).start()

    down_swap = remote(
        down, dn.at[pl.ds(HS, HS)], m_send.at[0], m_recv.at[0], sibling
    )
    down_swap.start()
    down_load.start()

    for cp in small_loads:
        cp.wait()
    here = lax.broadcasted_iota(jnp.int32, (MAXCH, E), 1) == z
    blocks = jnp.sum(jnp.where(here, list_ref[...], 0), axis=1, keepdims=True)
    count = jnp.sum(jnp.where(here[0:1], count_ref[...], 0), axis=1, keepdims=True)
    lane = lax.broadcasted_iota(jnp.int32, (8, LANE), 1)

    def targets(first_lane, first_unit):
        units = jnp.full((8, LANE), -1, jnp.int32)
        for j in range(MAXCH):
            start = first_lane + BLOCK_ROWS * j
            live = (lane >= start) & (lane < start + BLOCK_ROWS) & (count > j)
            unit = first_unit + 4 * (BLOCK_ROWS * blocks[j : j + 1, :] + lane - start)
            units = jnp.where(live, unit, units)
        return units.astype(F32)

    tgt[0] = targets(0, 0)
    tgt[1] = targets(CAP, HS)
    target_swap = remote(tgt.at[1], tgt.at[2], m_send.at[1], m_recv.at[1], sibling)
    target_swap.start()
    dn[pl.ds(2 * HS + 2 * CAP, 2 * CAP), :] = jnp.zeros((2 * CAP, D), BF16)

    row_ids = lax.broadcasted_iota(jnp.int32, (BLOCK_ROWS, 2 * CAP), 0)
    unit_ids = lax.broadcasted_iota(jnp.int32, (BLOCK_ROWS, 2 * CAP), 1)
    expert_lane = lax.broadcasted_iota(jnp.int32, (MAXCH, E), 1)

    def adam(e):
        wide = grad[e].astype(F32)
        top = BETA_ONE * one[e] + (1.0 - BETA_ONE) * wide
        bottom = BETA_TWO * two[e] + (1.0 - BETA_TWO) * wide * wide
        steps = -(LEARN_RATE * (top / FIRST_FIX) / (jnp.sqrt(bottom / SECOND_FIX) + ADAM_EPS))
        numbers = jnp.sum(
            jnp.where(expert_lane == e, list_ref[...], 0), axis=1, keepdims=True
        )
        taken = [
            jnp.where(unit_ids == BLOCK_ROWS * numbers[j : j + 1, :] + row_ids, 1.0, 0.0)
            for j in range(MAXCH)
        ]
        delta[e] = jnp.dot(
            jnp.concatenate(taken, axis=0).astype(BF16),
            steps.astype(BF16),
            preferred_element_type=F32,
        ).astype(BF16)

    for cp in adam_loads:
        cp.wait()

    @pl.loop(0, 4)
    def _(e):
        adam(e)

    start_group(0)

    @pl.loop(4, 8)
    def _(e):
        adam(e)

    start_group(1)

    delta_cols = pl.ds(pl.multiple_of(z * QUART, QUART), QUART)

    def d_copy(k):
        e = lax.rem(z + k, 8)
        return remote(
            delta.at[e],
            dn.at[pl.ds(2 * HS, CAP), delta_cols],
            d_send.at[k],
            d_recv.at[k],
            at(0, 0, k, c),
        )

    @pl.loop(1, 8)
    def _(k):
        d_copy(k).start()

    dn[pl.ds(2 * HS, CAP), delta_cols] = delta[z]
    spread(0)
    pass_on(0, 0)
    spread(1)
    pass_on(0, 1)

    def project(h, j, first):
        block = jnp.concatenate([xbuf[h, j, i] for i in range(4)], axis=1)
        for s in range(2):
            for g in range(2):
                parts = []
                for i in range(4):
                    a, b = i + h * (j - i), j + h * (i - j)
                    chip = 4 * lax.rem(x - a + 4, 4) + lax.rem(y - b + 4, 4)
                    rows = pl.ds(pl.multiple_of(chip * 2 * LANE + h * LANE, LANE), LANE)
                    parts.append(gu[s, g, rows, :])
                term = jnp.dot(
                    block, jnp.concatenate(parts, axis=0), preferred_element_type=F32
                )
                if first:
                    acc[2 * s + g] = term
                else:
                    acc[2 * s + g] += term

    @pl.loop(0, 8)
    def _(q):
        gu_load(q).wait()
        gu_swap(q).wait_recv()

    for g in range(2):
        for i in (1, 3, 2):
            pass_on(i, g)
    project(0, 0, True)
    project(1, 0, False)

    for k in range(1, 8):
        d_copy(k).wait_recv()
    delta_swap = remote(
        dn.at[pl.ds(2 * HS, CAP)],
        dn.at[pl.ds(2 * HS + CAP, CAP)],
        m_send.at[2],
        m_recv.at[2],
        sibling,
    )
    delta_swap.start()

    target_swap.wait_recv()
    unit = jnp.where(lane < CAP, tgt[0], tgt[2])[0:1, :]
    picks[...] = (
        lax.broadcasted_iota(jnp.int32, (2 * HS, LANE), 0).astype(F32) == unit
    ).astype(BF16)

    for step in range(2):
        hits, chosen = slots_of(step)
        w = weight_ref[step]
        by_expert = jnp.where(hits[0], w[0:1, :], 0.0) + jnp.where(hits[1], w[1:2, :], 0.0)
        full = jnp.concatenate(
            [jnp.where(chosen[e], by_expert[e : e + 1, :], 0.0) for e in range(E)], axis=0
        )
        full = full.T
        high = full.astype(BF16)
        mix[step, pl.ds(0, TOK), :] = high
        mix[step, pl.ds(TOK, TOK), :] = (full - high.astype(F32)).astype(BF16)

    @pl.loop(0, 4)
    def _(q):
        project(lax.rem(q, 2), 1 + 2 * (q // 2), False)

    for h in range(2):
        for i in range(4):
            for g in range(2):
                for w in range(2):
                    relay(h, w, i, g).wait_recv()
        project(h, 2, False)

    for s in range(2):
        gate = acc[2 * s]
        hid[:, pl.ds(s * HS, HS)] = (jax.nn.silu(gate) * acc[2 * s + 1]).astype(BF16)
    hid[:, pl.ds(2 * HS, LANE)] = jnp.dot(
        hid[:, pl.ds(0, 2 * HS)], picks[...], preferred_element_type=F32
    ).astype(BF16)

    down_load.wait()
    down_swap.wait_recv()
    delta_swap.wait_recv()

    def down_term(h, i):
        cols = []
        for j in range(4):
            a, b = i + h * (j - i), j + h * (i - j)
            block = 8 * lax.rem(x + a, 4) + 2 * lax.rem(y + b, 4) + h
            cols.append(dn[:, pl.ds(pl.multiple_of(block * LANE, LANE), LANE)])
        return jnp.dot(hid[...], jnp.concatenate(cols, axis=1), preferred_element_type=F32)

    def far_copy(h, w, b):
        return remote(
            far.at[h, pl.ds(w * HALF + (1 - b) * QROWS, QROWS), :],
            via.at[h, w, pl.ds((1 - b) * QROWS, QROWS), :],
            far_s.at[h, w, b],
            far_r.at[h, w, b],
            along(h, 1 + 2 * w),
        )

    def early_copy(h, w):
        rows = pl.ds((1 - w) * HALF, HALF)
        return remote(
            near.at[h, w, rows, :],
            came.at[h, w, rows, :],
            early_s.at[h, w],
            early_r.at[h, w],
            along(h, 1 + 2 * w),
        )

    def late_copy(h, w, b):
        rows = pl.ds(w * HALF + (1 - b) * QROWS, QROWS)
        return remote(
            near.at[h, w, rows, :],
            came.at[h, w, rows, :],
            late_s.at[h, w, b],
            late_r.at[h, w, b],
            along(h, 1 + 2 * w),
        )

    @pl.loop(0, 2)
    def _(h):
        far[h] = down_term(h, 2).astype(BF16)
        for b in range(2):
            for w in range(2):
                far_copy(h, w, b).start()

    for w in range(2):

        @pl.loop(0, 2)
        def _(h):
            term = down_term(h, 1 + 2 * w)
            direct = (1 - w) * HALF
            near[h, w, pl.ds(direct, HALF), :] = term[direct : direct + HALF].astype(BF16)
            early_copy(h, w).start()
            held[h, w] = term[w * HALF : (w + 1) * HALF]

    @pl.loop(0, 2)
    def _(h):
        own[h] = down_term(h, 0)

    for b in range(2):
        rows = pl.ds((1 - b) * QROWS, QROWS)
        for h in range(2):
            for w in range(2):
                far_copy(h, w, b).wait_recv()
                near[h, w, pl.ds(w * HALF + (1 - b) * QROWS, QROWS), :] = (
                    held[h, w, rows, :] + via[h, w, rows, :].astype(F32)
                ).astype(BF16)
                late_copy(h, w, b).start()

    def r2_copy(h, j, b):
        return remote(
            r2send.at[h, j - 1, b],
            r2recv.at[h, j - 1, b],
            r2s.at[h, j - 1, b],
            r2r.at[h, j - 1, b],
            along(1 - h, j),
        )

    for b in range(2):
        for h in range(2):
            for w in range(2):
                if b == 0:
                    early_copy(h, w).wait_recv()
                late_copy(h, w, b).wait_recv()
            for m in range(2):
                rows = pl.ds(m * HALF + (1 - b) * QROWS, QROWS)
                put = pl.ds(m * QROWS, QROWS)
                for j in (2, 1, 3, 0):
                    cols = pl.ds(j * LANE, LANE)
                    total = (
                        own[h, rows, cols]
                        + came[h, 0, rows, cols].astype(F32)
                        + came[h, 1, rows, cols].astype(F32)
                    )
                    if j:
                        r2send[h, j - 1, b, put, :] = total.astype(BF16)
                    else:
                        r2own[h, b, put, :] = total
            for j in (2, 1, 3):
                r2_copy(h, j, b).start()

    def r3_rows(n):
        return 1 - (n // 2) % 2, pl.ds((n % 2) * CAP + (n // 4) * QROWS, CAP)

    def r3_copy(h, n):
        b, rows = r3_rows(n)
        return remote(
            r3buf.at[h, b, rows, :],
            back.at[c, own_rows, :],
            r3s.at[n, h],
            r3r.at[n, c],
            at(0, 0, 8 - NEAR[n], h),
        )

    def r3_wait(step, n):
        rows = pl.ds(pl.multiple_of(lax.rem(z + NEAR[n], 8) * CAP, CAP), CAP)
        remote(
            back.at[step, rows, :],
            back.at[step, rows, :],
            r3s.at[n, step],
            r3r.at[n, step],
            at(0, 0, NEAR[n], step),
        ).wait_recv()

    for b in range(2):
        for h in range(2):
            for j in (1, 3, 2):
                r2_copy(h, j, b).wait_recv()
            total = r2own[h, b]
            for j in range(3):
                total += r2recv[h, j, b].astype(F32)
            r3buf[h, b] = total.astype(BF16)
            for n in (7, 6, 3, 2) if b == 0 else (5, 4, 1):
                r3_copy(h, n).start()
    r3_copy(1 - c, 0).start()
    b, rows = r3_rows(0)
    back[c, own_rows, :] = r3buf[c, b, rows, :]
    r3_wait(1 - c, 0)
    for step in range(2):
        for n in range(1, 8):
            r3_wait(step, n)
        both = jnp.dot(mix[step], back[step], preferred_element_type=F32)
        mixed[step] = (both[:TOK] + both[TOK:]).astype(BF16)

    r3_copy(1 - c, 0).wait_send()
    for n in range(1, 8):
        z_copy(n).wait_send()
        for h in range(2):
            r3_copy(h, n).wait_send()
    for h in range(2):
        for g in range(2):
            for i in range(4):
                if i:
                    first_copy(h, i, g).wait_send()
                for w in range(2):
                    second_copy(h, w, i, g).wait_send()
                    relay(h, w, i, g).wait_send()
        for w in range(2):
            early_copy(h, w).wait_send()
            for b in range(2):
                far_copy(h, w, b).wait_send()
                late_copy(h, w, b).wait_send()
        for j in range(1, 4):
            for b in range(2):
                r2_copy(h, j, b).wait_send()

    @pl.loop(0, 8)
    def _(q):
        gu_swap(q).wait_send()

    for k in range(1, 8):
        d_copy(k).wait_send()
    for cp in (down_swap, target_swap, delta_swap):
        cp.wait_send()


def experts(*args):
    hbm = pl.BlockSpec(memory_space=pltpu.HBM)
    dma = pltpu.SemaphoreType.DMA
    rows, cols = args[5].shape[1:]
    return pl.pallas_call(
        kernel,
        in_specs=[hbm] * 10,
        out_specs=pl.BlockSpec(memory_space=pltpu.VMEM),
        out_shape=pltpu.VMEM((2, TOK, LANE), BF16),
        scratch_shapes=[
            pltpu.VMEM((2, 2, TOK), jnp.int32),
            pltpu.VMEM((2, 2, TOK), F32),
            pltpu.VMEM((MAXCH, E), jnp.int32),
            pltpu.VMEM((1, E), jnp.int32),
            pltpu.VMEM((E, rows, cols), F32),
            pltpu.VMEM((E, rows, cols), F32),
            pltpu.VMEM((E, rows, cols), BF16),
            pltpu.VMEM((E, CAP, cols), BF16),
            pltpu.VMEM((TOK, 2 * LANE), BF16),
            pltpu.VMEM((2, SLOTS, LANE), BF16),
            pltpu.VMEM((2, 4, 4, SLOTS, LANE), BF16),
            pltpu.VMEM((2, 2, D, HS), BF16),
            pltpu.VMEM((KDOWN, D), BF16),
            pltpu.VMEM((4, SLOTS, HS), F32),
            pltpu.VMEM((SLOTS, KDOWN), BF16),
            pltpu.VMEM((2, 2 * TOK, SLOTS), BF16),
            pltpu.VMEM((3, 8, LANE), F32),
            pltpu.VMEM((2 * HS, LANE), BF16),
            pltpu.VMEM((2, SLOTS, QUART), BF16),
            pltpu.VMEM((2, 2, HALF, QUART), BF16),
            pltpu.VMEM((2, 2, SLOTS, QUART), BF16),
            pltpu.VMEM((2, 2, HALF, QUART), F32),
            pltpu.VMEM((2, 2, SLOTS, QUART), BF16),
            pltpu.VMEM((2, SLOTS, QUART), F32),
            pltpu.VMEM((2, 3, 2, HALF, LANE), BF16),
            pltpu.VMEM((2, 3, 2, HALF, LANE), BF16),
            pltpu.VMEM((2, 2, HALF, LANE), F32),
            pltpu.VMEM((2, 2, HALF, LANE), BF16),
            pltpu.VMEM((2, SLOTS, LANE), BF16),
            dma((9,)),
            dma((8,)),
            dma((3,)),
            dma((8,)),
            dma((8,)),
            dma((8,)),
            dma((8,)),
            dma((2, 4, 2)),
            dma((2, 4, 2)),
            dma((2, 2, 4, 2)),
            dma((2, 2, 4, 2)),
            dma((2, 2, 4, 2)),
            dma((2, 2, 4, 2)),
            dma((8,)),
            dma((8,)),
            dma((3,)),
            dma((3,)),
            dma((2, 2, 2)),
            dma((2, 2, 2)),
            dma((2, 2)),
            dma((2, 2)),
            dma((2, 2, 2)),
            dma((2, 2, 2)),
            dma((2, 3, 2)),
            dma((2, 3, 2)),
            dma((8, 2)),
            dma((8, 2)),
        ],
        compiler_params=pltpu.CompilerParams(
            collective_id=1, has_side_effects=True, vmem_limit_bytes=VMEM_BYTES
        ),
        cost_estimate=pl.CostEstimate(
            flops=3_600_000_000, bytes_accessed=12_000_000, transcendentals=400_000
        ),
        name="experts",
    )(*args)


def on_device(
    tokens,
    route,
    route_weight,
    gate_up,
    down_weight,
    adam_first,
    adam_second,
    gradient,
    block_list,
    block_count,
):
    inputs = (adam_first, adam_second, gradient)
    made = moments(True, *inputs)
    *made, tokens = lax.optimization_barrier((*made, tokens))
    mixed = experts(
        tokens,
        route.transpose(0, 2, 1),
        route_weight.transpose(0, 2, 1),
        gate_up[0],
        down_weight[0],
        adam_first,
        adam_second,
        gradient,
        block_list[:, 0, :].T,
        block_count.T,
    )
    *made, mixed = lax.optimization_barrier((*made, mixed))
    return mixed, *moments(False, *inputs, *made)


def solution(mesh):
    return jax.shard_map(
        on_device,
        mesh=mesh,
        in_specs=(
            P(None, "expert", None),
            P(None, "expert", None),
            P(None, "expert", None),
            P("expert", None, None, ("fsdp", "tensor")),
            P("expert", ("fsdp", "tensor"), None),
            P(None, ("fsdp", "tensor"), "expert"),
            P(None, ("fsdp", "tensor"), "expert"),
            P(None, ("fsdp", "tensor"), "expert"),
            P(None, ("fsdp", "tensor"), None),
            P(None, ("fsdp", "tensor")),
        ),
        out_specs=(
            P(None, "expert", ("fsdp", "tensor")),
            P(None, ("fsdp", "tensor"), "expert"),
            P(None, ("fsdp", "tensor"), "expert"),
        ),
        check_vma=False,
    )
```

time: 76.6 us -> 55.5 us (0.72)
  Pallas kernels: 68.5 us -> 54.1 us
  local copies, waits for them, and re-layouts: 7.08 us -> 0.62 us
    pallas_call x2 -> x3, Pallas kernels: 68.5 us -> 54.1 us  [the longest x1 50.9 us: experts(): pl.pallas_call(kernel, in_specs=[hbm] * 10, out_specs=pl.BlockSpec(memory...]
    unnamed x15 -> x1, local copies, waits for them, and re-layouts: 7.08 us -> 0.62 us
where the time goes in v2:
time: 55.5 us; the launch traced here: 55.4 us
  Pallas kernels  54.1 us (97%)
  between operations  0.65 us (1%)
  local copies, waits for them, and re-layouts  0.62 us (1%)
    pallas_call x1, Pallas kernels, experts(): pl.pallas_call(kernel, in_specs=[hbm] * 10, out_specs=pl.BlockSpec(memory...  50.9 us
    pallas_call x2, Pallas kernels, moments(): pl.pallas_call(functools.partial(moments_kernel, first_part), in_specs=[h...  3.2 us

profile of v2, /device:TPU:1, one launch (start us, length us, event | category | flops | bytes accessed | tf_op | source)
XLA Modules:
  0.0 55.4 jit_solution(15147653629389789340)
XLA Ops:
  0.6 2.8 %moments_first.1 = (f32[8,64,512]{2,1,0:T(8,128)}, f32[8,64,512]{2,1,0:T(8,128)}) custom-call(f32[8,64,512]{2,1,0:T(8,128)} %m_in.3, f32[8,64,512]{2,1,0:T(8,128)} %v_in.3, bf16[8,64,512]{2,1,0:T(8,128)(2,1)} %g_in.3), custom_call_target="tpu_custom_call" | custom-call | tf_op jit(solution)/shard_map/moments_first/pallas_call | solution.py:78
  3.5 50.9 %experts.1 = bf16[2,64,128]{2,1,0:T(8,128)(2,1)S(1)} custom-call(bf16[2,64,4096]{2,1,0:T(8,128)(2,1)} %tokens, s32[2,2,64]{2,1,0:T(2,128)} %bitcast.10, f32[2,2,64]{2,1,0:T(2,128)} %bitcast.11, bf16[2,4096,256]{2,1,0:T(8,128)(2,1)} %bitcast.8, bf16[256,4096]{1,0:T(8,128)(2,1)} %bitcast.9, f32[8,64,512]{2,1,0:T(8,128)} %m_in.3, f32[8,64,512]{2,1,0:T(8,128)} %v_in.3, ...), custom_call_target="tpu_custom_call" | custom-call | flops 3600000000 | bytes 12000000 | tf_op jit(solution)/shard_map/experts/pallas_call | solution.py:680
  54.4 0.6 %copy.18 = bf16[2,64,128]{2,1,0:T(8,128)(2,1)} copy(bf16[2,64,128]{2,1,0:T(8,128)(2,1)S(1)} %experts.1) | data formatting | bytes 65536
  55.0 0.4 moments_last.1

commit v3 on v2

--- a/solution.py
+++ b/solution.py
@@ -23,6 +23,8 @@
 LANE = 128
 KDOWN = 2 * HS + 128
 NEAR = (0, 1, 7, 2, 6, 3, 5, 4)
+WIDE = 1
+GROUPS = ((1, 5), (5, 8))
 HALF = 128
 QROWS = 64
 LOW = 3
@@ -113,6 +115,9 @@
     grad,
     delta,
     tok,
+    full,
+    selector,
+    wide,
     zsend,
     xbuf,
     gu,
@@ -140,6 +145,8 @@
     sib_recv,
     z_send,
     z_recv,
+    w_send,
+    w_recv,
     p_send,
     p_recv,
     f_send,
@@ -203,6 +210,7 @@
     route_load = small(route_in, route_ref, 4)
     columns = pl.ds(pl.multiple_of((4 * x + y) * 2 * LANE, 2 * LANE), 2 * LANE)
     tok_load = small(tokens.at[c, :, columns], tok, 0)
+    full_load = small(tokens.at[c], full, 1)
     small_loads = [
         small(list_in, list_ref, 6),
         small(count_in, count_ref, 7),
@@ -213,7 +221,7 @@
         for n, (src, dst) in enumerate(((moment_one, one), (moment_two, two), (gradient, grad)))
     ]
     down_load = small(down, dn.at[pl.ds(0, HS)], 2)
-    for cp in [route_load, tok_load] + small_loads + adam_loads:
+    for cp in [route_load, tok_load, full_load] + small_loads + adam_loads:
         cp.start()
 
     def gu_load(q):
@@ -239,32 +247,53 @@
 
     route_load.wait()
     _, chosen = slots_of(c)
-    selector = jnp.concatenate([jnp.where(m, 1.0, 0.0) for m in chosen], axis=0).astype(BF16)
+    selector[...] = jnp.concatenate(
+        [jnp.where(m, 1.0, 0.0) for m in chosen], axis=0
+    ).astype(BF16)
     tok_load.wait()
-    picked = jnp.dot(selector, tok[...], preferred_element_type=F32).astype(BF16)
+    picked = jnp.dot(selector[...], tok[...], preferred_element_type=F32).astype(BF16)
     for h in range(2):
         zsend[h] = picked[:, h * LANE : (h + 1) * LANE]
-    own_rows = pl.ds(pl.multiple_of(z * CAP, CAP), CAP)
-    for h in range(2):
-        xbuf[h, 0, 0, pl.ds(0, CAP), :] = zsend[h, own_rows, :]
+
+    def expert_rows(n):
+        return pl.ds(pl.multiple_of(lax.rem(z + NEAR[n], 8) * CAP, CAP), CAP)
+
+    own_rows = expert_rows(0)
 
     pl.semaphore_wait(barrier, 21)
 
     def z_copy(n):
-        rows = pl.ds(pl.multiple_of(lax.rem(z + NEAR[n], 8) * CAP, CAP), CAP)
-        return remote(
-            zsend.at[:, rows, :],
+        return remote(
+            zsend.at[:, expert_rows(n), :],
             xbuf.at[:, 0, 0, pl.ds(n * CAP, CAP), :],
             z_send.at[n],
             z_recv.at[n],
             at(0, 0, NEAR[n], c),
         )
 
-    for n in range(1, 8):
+    def wide_copy(n, h):
+        return remote(
+            wide.at[n - 1, h],
+            xbuf.at[h, :, :, pl.ds(n * CAP, CAP), :],
+            w_send.at[n, h],
+            w_recv.at[n, h],
+            at(0, 0, NEAR[n], c),
+        )
+
+    for n in range(7, WIDE - 1, -1):
         z_copy(n).start()
 
+    def group(g):
+        start, end = GROUPS[g]
+        return pl.ds(start * CAP, (end - start) * CAP)
+
+    def half_group(g, w):
+        start, end = GROUPS[g]
+        size = (end - start) * CAP // 2
+        return pl.ds(start * CAP + w * size, size)
+
     def first_copy(h, i, g):
-        rows = pl.ds(g * HALF, HALF)
+        rows = group(g)
         return remote(
             xbuf.at[h, 0, 0, rows, :],
             xbuf.at[h, 0, i, rows, :],
@@ -274,7 +303,7 @@
         )
 
     def second_copy(h, w, i, g):
-        rows = pl.ds(g * HALF, HALF)
+        rows = group(g)
         return remote(
             xbuf.at[h, 0, i, rows, :],
             xbuf.at[h, 1 + 2 * w, i, rows, :],
@@ -284,7 +313,7 @@
         )
 
     def relay(h, w, i, g):
-        rows = pl.ds(g * HALF + w * QROWS, QROWS)
+        rows = half_group(g, w)
         return remote(
             xbuf.at[h, 1 + 2 * w, i, rows, :],
             xbuf.at[h, 2, i, rows, :],
@@ -294,14 +323,14 @@
         )
 
     def start_group(g):
-        for n in range(4 * g, 4 * g + 4):
-            if n:
-                z_copy(n).wait_recv()
+        for n in range(*GROUPS[g]):
+            z_copy(n).wait_recv()
+        for i in (2, 1, 3):
+            for h in range(2):
+                first_copy(h, i, g).start()
         for h in range(2):
             for w in range(2):
-                first_copy(h, 1 + 2 * w, g).start()
                 second_copy(h, w, 0, g).start()
-            first_copy(h, 2, g).start()
 
     def spread(g):
         for i in (1, 3, 2):
@@ -394,8 +423,6 @@
     def _(e):
         adam(e)
 
-    start_group(1)
-
     delta_cols = pl.ds(pl.multiple_of(z * QUART, QUART), QUART)
 
     def d_copy(k):
@@ -413,6 +440,36 @@
         d_copy(k).start()
 
     dn[pl.ds(2 * HS, CAP), delta_cols] = delta[z]
+    start_group(1)
+
+    full_load.wait()
+
+    @pl.loop(0, 8)
+    def _(q):
+        h, j = q // 4, lax.rem(q, 4)
+        parts = []
+        for i in range(4):
+            a, b = i + h * (j - i), j + h * (i - j)
+            chip = 4 * lax.rem(x - a + 4, 4) + lax.rem(y - b + 4, 4)
+            start = pl.multiple_of(chip * 2 * LANE + h * LANE, LANE)
+            parts.append(full[:, pl.ds(start, LANE)])
+        block = jnp.concatenate(parts, axis=1)
+        for n in range(WIDE):
+            rows = jnp.dot(
+                selector[expert_rows(n), :], block, preferred_element_type=F32
+            ).astype(BF16)
+            for i in range(4):
+                piece = rows[:, i * LANE : (i + 1) * LANE]
+                if n:
+                    wide[n - 1, h, j, i] = piece
+                else:
+                    xbuf[h, j, i, pl.ds(0, CAP), :] = piece
+
+    for n in range(1, WIDE):
+        for h in range(2):
+            wide_copy(n, h).start()
+
+
     spread(0)
     pass_on(0, 0)
     spread(1)
@@ -444,6 +501,9 @@
     for g in range(2):
         for i in (1, 3, 2):
             pass_on(i, g)
+    for n in range(1, WIDE):
+        for h in range(2):
+            wide_copy(n, h).wait_recv()
     project(0, 0, True)
     project(1, 0, False)
 
@@ -565,6 +625,29 @@
                     held[h, w, rows, :] + via[h, w, rows, :].astype(F32)
                 ).astype(BF16)
                 late_copy(h, w, b).start()
+
+    for n in range(WIDE, 8):
+        z_copy(n).wait_send()
+    for n in range(1, WIDE):
+        for h in range(2):
+            wide_copy(n, h).wait_send()
+    for h in range(2):
+        for g in range(2):
+            for i in range(4):
+                if i:
+                    first_copy(h, i, g).wait_send()
+                for w in range(2):
+                    second_copy(h, w, i, g).wait_send()
+                    relay(h, w, i, g).wait_send()
+
+    @pl.loop(0, 8)
+    def _(q):
+        gu_swap(q).wait_send()
+
+    for k in range(1, 8):
+        d_copy(k).wait_send()
+    for cp in (down_swap, target_swap, delta_swap):
+        cp.wait_send()
 
     def r2_copy(h, j, b):
         return remote(
@@ -598,6 +681,13 @@
             for j in (2, 1, 3):
                 r2_copy(h, j, b).start()
 
+    for h in range(2):
+        for w in range(2):
+            early_copy(h, w).wait_send()
+            for b in range(2):
+                far_copy(h, w, b).wait_send()
+                late_copy(h, w, b).wait_send()
+
     def r3_rows(n):
         return 1 - (n // 2) % 2, pl.ds((n % 2) * CAP + (n // 4) * QROWS, CAP)
 
@@ -634,6 +724,10 @@
     r3_copy(1 - c, 0).start()
     b, rows = r3_rows(0)
     back[c, own_rows, :] = r3buf[c, b, rows, :]
+    for h in range(2):
+        for j in range(1, 4):
+            for b in range(2):
+                r2_copy(h, j, b).wait_send()
     r3_wait(1 - c, 0)
     for step in range(2):
         for n in range(1, 8):
@@ -643,34 +737,8 @@
 
     r3_copy(1 - c, 0).wait_send()
     for n in range(1, 8):
-        z_copy(n).wait_send()
         for h in range(2):
             r3_copy(h, n).wait_send()
-    for h in range(2):
-        for g in range(2):
-            for i in range(4):
-                if i:
-                    first_copy(h, i, g).wait_send()
-                for w in range(2):
-                    second_copy(h, w, i, g).wait_send()
-                    relay(h, w, i, g).wait_send()
-        for w in range(2):
-            early_copy(h, w).wait_send()
-            for b in range(2):
-                far_copy(h, w, b).wait_send()
-                late_copy(h, w, b).wait_send()
-        for j in range(1, 4):
-            for b in range(2):
-                r2_copy(h, j, b).wait_send()
-
-    @pl.loop(0, 8)
-    def _(q):
-        gu_swap(q).wait_send()
-
-    for k in range(1, 8):
-        d_copy(k).wait_send()
-    for cp in (down_swap, target_swap, delta_swap):
-        cp.wait_send()
 
 
 def experts(*args):
@@ -692,6 +760,9 @@
             pltpu.VMEM((E, rows, cols), BF16),
             pltpu.VMEM((E, CAP, cols), BF16),
             pltpu.VMEM((TOK, 2 * LANE), BF16),
+            pltpu.VMEM((TOK, D), BF16),
+            pltpu.VMEM((SLOTS, TOK), BF16),
+            pltpu.VMEM((2, 2, 4, 4, CAP, LANE), BF16),
             pltpu.VMEM((2, SLOTS, LANE), BF16),
             pltpu.VMEM((2, 4, 4, SLOTS, LANE), BF16),
             pltpu.VMEM((2, 2, D, HS), BF16),
@@ -719,6 +790,8 @@
             dma((8,)),
             dma((8,)),
             dma((8,)),
+            dma((3, 2)),
+            dma((3, 2)),
             dma((2, 4, 2)),
             dma((2, 4, 2)),
             dma((2, 2, 4, 2)),

time: 55.5 us -> 54.5 us (0.982)
  Pallas kernels: 54.1 us -> 53.2 us
    pallas_call x1, Pallas kernels: 50.9 us -> 50 us  [experts(): pl.pallas_call(kernel, in_specs=[hbm] * 10, out_specs=pl.BlockSpec(memory...]
where the time goes in v3:
time: 54.5 us; the launch traced here: 54.4 us
  Pallas kernels  53.2 us (98%)
  between operations  0.65 us (1%)
  local copies, waits for them, and re-layouts  0.62 us (1%)
    pallas_call x1, Pallas kernels, experts(): pl.pallas_call(kernel, in_specs=[hbm] * 10, out_specs=pl.BlockSpec(memory...  50 us
    pallas_call x2, Pallas kernels, moments(): pl.pallas_call(functools.partial(moments_kernel, first_part), in_specs=[h...  3.2 us

profile of v3, /device:TPU:1, one launch (start us, length us, event | category | flops | bytes accessed | tf_op | source)
XLA Modules:
  0.0 54.4 jit_solution(5130533331184826348)
XLA Ops:
  0.6 2.8 %moments_first.1 = (f32[8,64,512]{2,1,0:T(8,128)}, f32[8,64,512]{2,1,0:T(8,128)}) custom-call(f32[8,64,512]{2,1,0:T(8,128)} %m_in.3, f32[8,64,512]{2,1,0:T(8,128)} %v_in.3, bf16[8,64,512]{2,1,0:T(8,128)(2,1)} %g_in.3), custom_call_target="tpu_custom_call" | custom-call | tf_op jit(solution)/shard_map/moments_first/pallas_call | solution.py:80
  3.5 50.0 %experts.1 = bf16[2,64,128]{2,1,0:T(8,128)(2,1)S(1)} custom-call(bf16[2,64,4096]{2,1,0:T(8,128)(2,1)} %tokens, s32[2,2,64]{2,1,0:T(2,128)} %bitcast.10, f32[2,2,64]{2,1,0:T(2,128)} %bitcast.11, bf16[2,4096,256]{2,1,0:T(8,128)(2,1)} %bitcast.8, bf16[256,4096]{1,0:T(8,128)(2,1)} %bitcast.9, f32[8,64,512]{2,1,0:T(8,128)} %m_in.3, f32[8,64,512]{2,1,0:T(8,128)} %v_in.3, ...), custom_call_target="tpu_custom_call" | custom-call | flops 3600000000 | bytes 12000000 | tf_op jit(solution)/shard_map/experts/pallas_call | solution.py:748
  53.4 0.6 %copy.18 = bf16[2,64,128]{2,1,0:T(8,128)(2,1)} copy(bf16[2,64,128]{2,1,0:T(8,128)(2,1)S(1)} %experts.1) | data formatting | bytes 65536
  54.1 0.4 moments_last.1

commit v4 on v3

--- a/solution.py
+++ b/solution.py
@@ -24,7 +24,7 @@
 KDOWN = 2 * HS + 128
 NEAR = (0, 1, 7, 2, 6, 3, 5, 4)
 WIDE = 1
-GROUPS = ((1, 5), (5, 8))
+GROUPS = ((1, 4), (4, 8))
 HALF = 128
 QROWS = 64
 LOW = 3
@@ -612,10 +612,6 @@
             early_copy(h, w).start()
             held[h, w] = term[w * HALF : (w + 1) * HALF]
 
-    @pl.loop(0, 2)
-    def _(h):
-        own[h] = down_term(h, 0)
-
     for b in range(2):
         rows = pl.ds((1 - b) * QROWS, QROWS)
         for h in range(2):
@@ -625,6 +621,10 @@
                     held[h, w, rows, :] + via[h, w, rows, :].astype(F32)
                 ).astype(BF16)
                 late_copy(h, w, b).start()
+
+    @pl.loop(0, 2)
+    def _(h):
+        own[h] = down_term(h, 0)
 
     for n in range(WIDE, 8):
         z_copy(n).wait_send()

time: 54.5 us -> 54.3 us (level)
  no operation moved by 1% of the time
where the time goes in v4:
time: 54.3 us; the launch traced here: 54.2 us
  Pallas kernels  52.9 us (97%)
  between operations  0.65 us (1%)
  local copies, waits for them, and re-layouts  0.62 us (1%)
    pallas_call x1, Pallas kernels, experts(): pl.pallas_call(kernel, in_specs=[hbm] * 10, out_specs=pl.BlockSpec(memory...  49.7 us
    pallas_call x2, Pallas kernels, moments(): pl.pallas_call(functools.partial(moments_kernel, first_part), in_specs=[h...  3.2 us

profile of v4, /device:TPU:1, one launch (start us, length us, event | category | flops | bytes accessed | tf_op | source)
XLA Modules:
  0.0 54.2 jit_solution(7416569954415537646)
XLA Ops:
  0.6 2.8 %moments_first.1 = (f32[8,64,512]{2,1,0:T(8,128)}, f32[8,64,512]{2,1,0:T(8,128)}) custom-call(f32[8,64,512]{2,1,0:T(8,128)} %m_in.3, f32[8,64,512]{2,1,0:T(8,128)} %v_in.3, bf16[8,64,512]{2,1,0:T(8,128)(2,1)} %g_in.3), custom_call_target="tpu_custom_call" | custom-call | tf_op jit(solution)/shard_map/moments_first/pallas_call | solution.py:80
  3.5 49.7 %experts.1 = bf16[2,64,128]{2,1,0:T(8,128)(2,1)S(1)} custom-call(bf16[2,64,4096]{2,1,0:T(8,128)(2,1)} %tokens, s32[2,2,64]{2,1,0:T(2,128)} %bitcast.10, f32[2,2,64]{2,1,0:T(2,128)} %bitcast.11, bf16[2,4096,256]{2,1,0:T(8,128)(2,1)} %bitcast.8, bf16[256,4096]{1,0:T(8,128)(2,1)} %bitcast.9, f32[8,64,512]{2,1,0:T(8,128)} %m_in.3, f32[8,64,512]{2,1,0:T(8,128)} %v_in.3, ...), custom_call_target="tpu_custom_call" | custom-call | flops 3600000000 | bytes 12000000 | tf_op jit(solution)/shard_map/experts/pallas_call | solution.py:748
  53.2 0.6 %copy.18 = bf16[2,64,128]{2,1,0:T(8,128)(2,1)} copy(bf16[2,64,128]{2,1,0:T(8,128)(2,1)S(1)} %experts.1) | data formatting | bytes 65536
  53.8 0.4 moments_last.1
